TPU v7x, 128 devices: a whole 4x4x4 slice. The times are simulated.
128 devices in a mesh: gx: 8 (over z, core), gy: 16 (over y, x).
Axes of the slice: x: 4, y: 4, z: 4, core: 2. Of those that a mesh axis runs over, the one named last changes fastest.
Arguments:
- tokens: bfloat16 [512, 8192], P('gy', 'gx'), may hold values from -7 to 7
- gain: float32 [8192], P('gx'), may hold values from 0.1 to 1.9
- gate_weight: bfloat16 [8192, 32768], P('gx', 'gy'), may hold values from -0.0625 to 0.0625
- up_weight: bfloat16 [8192, 32768], P('gx', 'gy'), may hold values from -0.0625 to 0.0625
- down_weight: bfloat16 [32768, 8192], P('gy', 'gx'), may hold values from -0.03125 to 0.03125
- query_weight: bfloat16 [8192, 8192], P('gx', 'gy'), may hold values from -0.0625 to 0.0625
- pair_weight: bfloat16 [8192, 512], P('gx', 'gy'), may hold values from -0.0625 to 0.0625
- out_weight: bfloat16 [8192, 8192], P('gy', 'gx'), may hold values from -0.0625 to 0.0625
- cache_k: bfloat16 [512, 1024, 256], P(('gx', 'gy')), may hold values from -360 to 360
- cache_v: bfloat16 [512, 1024, 256], P(('gx', 'gy')), may hold values from -6 to 6
- lengths: int32 [512], P('gx'), may hold values from 1 to 1024, as said below
Outputs:
- mixed: bfloat16 [512, 8192], P('gy', 'gx')
- new_pair: bfloat16 [512, 512], P(('gx', 'gy'))
Inputs may be any that keep to these rules, and one draw needn't show every extreme that they name: `lengths`: each row has at least one cached token; the largest length equals 1024 in every draw. Cache slots at a row's length and beyond hold no history.
All inputs are finite; a program needn't handle non-finite values.
Results may differ from a plain program's by a relative error of at most 0.0093.
Values may be sent and summed in bfloat16 or wider, within the bound.
A program may use at most 128 MiB of HBM per device.

v0:
```python
import jax
import jax.numpy as jnp
from jax import lax
from jax.sharding import PartitionSpec as P

EPS = 1e-05


def rotate_pairs(values, positions, first_pair, head, limit):
    rows, cols = values.shape
    pairs = values.reshape(rows, cols // 2, 2)
    index = first_pair + jnp.arange(cols // 2, dtype=jnp.int32)
    slot = (index % (head // 2)).astype(jnp.float32)
    freq = jnp.power(10000.0, -2.0 * slot / head)
    angle = positions.astype(jnp.float32)[:, None] * freq[None, :]
    cosine = jnp.cos(angle)
    sine = jnp.sin(angle)
    even = pairs[:, :, 0]
    odd = pairs[:, :, 1]
    turned = jnp.stack([even * cosine - odd * sine, even * sine + odd * cosine], axis=-1)
    keep = (2 * index < limit)[None, :, None]
    return jnp.where(keep, turned, pairs).reshape(rows, cols)


def attend(query, new_pair, cache_k, cache_v, own_lengths):
    rows, width = query.shape
    slots = cache_k.shape[1]
    head = cache_k.shape[2]
    heads = width // head
    heads_q = query.reshape(rows, heads, head)
    new_key = new_pair[:, :head]
    new_value = new_pair[:, head:]
    scale = head ** (-0.5)
    scores = (
        jnp.einsum("rhd,rld->rhl", heads_q, cache_k, preferred_element_type=jnp.float32) * scale
    )
    fresh = jnp.einsum("rhd,rd->rh", heads_q, new_key, preferred_element_type=jnp.float32) * scale
    valid = jnp.arange(slots, dtype=jnp.int32)[None, None, :] < own_lengths[:, None, None]
    top = jnp.maximum(jnp.max(jnp.where(valid, scores, -1e30), axis=2), fresh)
    weights = jnp.where(valid, jnp.exp(scores - top[:, :, None]), 0.0)
    fresh_weight = jnp.exp(fresh - top)
    total = jnp.sum(weights, axis=2) + fresh_weight
    probs = (weights / total[:, :, None]).astype(jnp.bfloat16)
    fresh_prob = (fresh_weight / total).astype(jnp.bfloat16)
    attended = jnp.einsum("rhl,rld->rhd", probs, cache_v, preferred_element_type=jnp.float32)
    attended = (
        attended
        + fresh_prob.astype(jnp.float32)[:, :, None] * new_value.astype(jnp.float32)[:, None, :]
    )
    return attended.astype(jnp.bfloat16).reshape(rows, heads * head)


def local(
    tokens,
    gain,
    gate_weight,
    up_weight,
    down_weight,
    query_weight,
    pair_weight,
    out_weight,
    cache_k,
    cache_v,
    lengths,
):
    width = tokens.shape[1] * lax.axis_size("gx")
    head = cache_k.shape[2]
    values = tokens.astype(jnp.float32)
    mean = lax.psum(jnp.sum(values, axis=1), "gx") / width
    centered = values - mean[:, None]
    spread = lax.psum(jnp.sum(centered * centered, axis=1), "gx") / width
    normed = (centered * lax.rsqrt(spread + EPS)[:, None] * gain[None, :]).astype(jnp.bfloat16)
    gathered = lax.all_gather(normed, "gy", axis=0, tiled=True)
    gate_part = jnp.dot(gathered, gate_weight, preferred_element_type=jnp.float32)
    up_part = jnp.dot(gathered, up_weight, preferred_element_type=jnp.float32)
    query_part = jnp.dot(gathered, query_weight, preferred_element_type=jnp.float32)
    pair_part = jnp.dot(gathered, pair_weight, preferred_element_type=jnp.float32)
    col_block = lax.axis_index("gy")
    gate, up, query, pair = (
        lax.psum_scatter(gate_part, "gx", scatter_dimension=0, tiled=True),
        lax.psum_scatter(up_part, "gx", scatter_dimension=0, tiled=True),
        lax.psum_scatter(query_part, "gx", scatter_dimension=0, tiled=True),
        lax.psum_scatter(pair_part, "gx", scatter_dimension=0, tiled=True),
    )
    hidden = (jax.nn.silu(gate) * up).astype(jnp.bfloat16)
    query_turned = rotate_pairs(query, lengths, 0, head, query.shape[1]).astype(jnp.bfloat16)
    first_pair = col_block * (pair.shape[1] // 2)
    pair_turned = rotate_pairs(pair, lengths, first_pair, head, head).astype(jnp.bfloat16)
    query_own, pair_own = (
        lax.all_to_all(query_turned, "gy", split_axis=0, concat_axis=1, tiled=True),
        lax.all_to_all(pair_turned, "gy", split_axis=0, concat_axis=1, tiled=True),
    )
    owned = query_own.shape[0]
    own_lengths = lax.dynamic_slice_in_dim(lengths, col_block * owned, owned, 0)
    attended = attend(query_own, pair_own, cache_k, cache_v, own_lengths)
    returned = lax.all_to_all(attended, "gy", split_axis=1, concat_axis=0, tiled=True)
    ff_cols = down_weight.shape[0]
    joined = jnp.concatenate([hidden, returned], axis=1)
    piece = lax.all_gather(joined, "gx", axis=0, tiled=True)
    terms = jnp.dot(piece[:, :ff_cols], down_weight, preferred_element_type=jnp.float32) + jnp.dot(
        piece[:, ff_cols:], out_weight, preferred_element_type=jnp.float32
    )
    summed = lax.psum_scatter(terms, "gy", scatter_dimension=0, tiled=True)
    mixed = (summed + values).astype(jnp.bfloat16)
    return (mixed, pair_own)


def solution(mesh):
    in_specs = (
        P("gy", "gx"),
        P("gx"),
        P("gx", "gy"),
        P("gx", "gy"),
        P("gy", "gx"),
        P("gx", "gy"),
        P("gx", "gy"),
        P("gy", "gx"),
        P(("gx", "gy"), None, None),
        P(("gx", "gy"), None, None),
        P("gx"),
    )
    out_specs = (P("gy", "gx"), P(("gx", "gy"), None))
    return jax.shard_map(local, mesh=mesh, in_specs=in_specs, out_specs=out_specs, check_vma=False)
```

profile of v0, /device:TPU:1, one launch (start us, length us, event | category | flops | bytes accessed | tf_op | source)
XLA Modules:
  0.0 343.6 jit_solution(13085149530580952379)
XLA Ops:
  7.2 0.0 all-gather.3.cloned.1.call-start
  7.2 1.1 convert_reduce_fusion
  8.3 14.5 %psum.14 = f32[32]{0:T(128)S(1)} all-reduce(f32[32]{0:T(128)S(1)} %convert_reduce_fusion), channel_id=1, replica_groups=mesh['gx'=8,'gy'=16] {'gx'}, use_global_device_ids=true, to_apply=%region_1.0 | all-reduce | flops 32 | bytes 256 | tf_op jit(solution)/shard_map/psum | solution.py:69
  22.8 1.0 fusion.11
  23.8 14.7 %psum.15 = f32[32]{0:T(128)S(1)} all-reduce(f32[32]{0:T(128)S(1)} %fusion.11), channel_id=1, replica_groups=mesh['gx'=8,'gy'=16] {'gx'}, use_global_device_ids=true, to_apply=%region_3.0 | all-reduce | flops 32 | bytes 256 | tf_op jit(solution)/shard_map/psum | solution.py:71
  38.5 1.6 fusion.13
  40.1 0.0 reduce-scatter.16.cloned.1.call-start
  40.2 40.1 %all-gather.3.cloned.1.call-done = bf16[512,1024]{1,0:T(8,128)(2,1)} async-done(((bf16[32,1024]{1,0:T(8,128)(2,1)}), bf16[512,1024]{1,0:T(8,128)(2,1)}) %all-gather.3.cloned.1.call-update) | async-done | bytes 1048592 | tf_op jit(solution)/shard_map/all_gather | solution.py:73
  80.3 2.3 fusion.44
  82.6 0.0 reduce-scatter.16.cloned.1.call-update
  82.7 0.0 reduce-scatter.12.cloned.1.call-start
  82.7 3.4 fusion.43
  86.1 0.0 reduce-scatter.12.cloned.1.call-update
  86.1 0.0 reduce-scatter.10.cloned.1.call-start
  86.2 6.5 %fusion.42 = f32[512,2048]{1,0:T(8,128)} fusion(bf16[512,1024]{1,0:T(8,128)(2,1)S(1)} %copy-done.1, bf16[1024,2048]{1,0:T(8,128)(2,1)} %param.14), kind=kOutput, calls=%fused_computation.76 | convolution fusion | flops 2147483648 | bytes 9437184 | tf_op jit(solution)/shard_map/dot_general | solution.py:75
  92.6 0.0 reduce-scatter.10.cloned.1.call-update
  92.7 0.0 reduce-scatter.8.cloned.1.call-start
  92.7 6.5 %fusion.41 = f32[512,2048]{1,0:T(8,128)} fusion(bf16[512,1024]{1,0:T(8,128)(2,1)S(1)} %copy-done.1, bf16[1024,2048]{1,0:T(8,128)(2,1)} %param.13), kind=kOutput, calls=%fused_computation.75 | convolution fusion | flops 2147483648 | bytes 9437184 | tf_op jit(solution)/shard_map/dot_general | solution.py:74
  99.2 0.6 copy-done.6
  99.9 0.1 dynamic_slice.3
  100.0 0.1 broadcast_in_dim.62
  100.0 0.1 broadcast_in_dim.63
  100.2 0.1 iota_compare_fusion
  100.2 11.2 %reduce-scatter.16.cloned.1.call-done = f32[64,32]{1,0:T(8,128)} async-done(((f32[512,32]{1,0:T(8,128)}), f32[64,32]{1,0:T(8,128)}) %reduce-scatter.16.cloned.1.call-update) | async-done | bytes 8208
  111.4 0.8 copy.66
  112.3 0.1 fusion.25
  112.4 0.1 select_convert_fusion.1
  112.5 0.7 copy.60
  113.2 6.5 %all-to-all-start.1 = ((bf16[16,4,32]{2,1,0:T(4,128)(2,1)}), bf16[16,4,32]{2,1,0:T(4,128)(2,1)S(1)}, u32[]{:S(2)}, u32[]{:S(2)}) async-start(bf16[16,4,32]{2,1,0:T(4,128)(2,1)} %bitcast.5), calls=%async_computation.4 | async-start | bytes 32768 | tf_op jit(solution)/shard_map/all_to_all | solution.py:91
  119.7 0.1 broadcast_in_dim.58
  119.9 0.2 broadcast_in_dim.59
  120.0 6.2 %all-to-all-done.1 = bf16[16,4,32]{2,1,0:T(4,128)(2,1)S(1)} async-done(((bf16[16,4,32]{2,1,0:T(4,128)(2,1)}), bf16[16,4,32]{2,1,0:T(4,128)(2,1)S(1)}, u32[]{:S(2)}, u32[]{:S(2)}) %all-to-all-start.1) | async-done | bytes 4128 | tf_op jit(solution)/shard_map/all_to_all | solution.py:91
  126.2 0.1 all_to_all.46
  126.3 18.4 %reduce-scatter.12.cloned.1.call-done = f32[64,512]{1,0:T(8,128)} async-done(((f32[512,512]{1,0:T(8,128)}), f32[64,512]{1,0:T(8,128)}) %reduce-scatter.12.cloned.1.call-update) | async-done | bytes 131088 | tf_op jit(solution)/shard_map/reduce_scatter | solution.py:82
  144.7 1.0 copy.51
  145.7 0.2 fusion.39
  145.9 0.1 copy.68
  146.0 0.1 copy.67
  146.1 0.3 fusion.19
  146.4 0.1 copy.54
  146.6 0.1 copy.55
  146.7 0.9 select_convert_fusion
  147.6 0.7 all_to_all.40
  148.2 6.5 %all-to-all-start = ((bf16[16,4,512]{2,1,0:T(4,128)(2,1)}), bf16[16,4,512]{2,1,0:T(4,128)(2,1)S(1)}, u32[]{:S(2)}, u32[]{:S(2)}) async-start(bf16[16,4,512]{2,1,0:T(4,128)(2,1)} %all_to_all.40), calls=%async_computation.3 | async-start | bytes 131072 | tf_op jit(solution)/shard_map/all_to_all | solution.py:90
  154.8 0.0 all-gather.5.cloned.1.call-start
  154.9 6.5 %all-to-all-done = bf16[16,4,512]{2,1,0:T(4,128)(2,1)S(1)} async-done(((bf16[16,4,512]{2,1,0:T(4,128)(2,1)}), bf16[16,4,512]{2,1,0:T(4,128)(2,1)S(1)}, u32[]{:S(2)}, u32[]{:S(2)}) %all-to-all-start) | async-done | bytes 65568 | tf_op jit(solution)/shard_map/all_to_all | solution.py:90
  161.4 0.1 fusion.27
  161.5 0.8 select_reduce_fusion
  162.3 0.3 fusion.4
  162.6 0.4 copy-done.5
  163.0 0.5 fusion.2
  163.5 0.1 copy.62
  163.6 9.4 %all_to_all.54 = bf16[4,16,512]{2,0,1:T(4,128)(2,1)S(1)} all-to-all(bf16[4,16,512]{2,0,1:T(4,128)(2,1)S(1)} %copy.62), channel_id=1, replica_groups=mesh['gx'=8,'gy'=16] {'gy'}, dimensions={1} | all-to-all | bytes 131072 | tf_op jit(solution)/shard_map/all_to_all | solution.py:96
  173.0 11.1 %reduce-scatter.10.cloned.1.call-done = f32[64,2048]{1,0:T(8,128)} async-done(((f32[512,2048]{1,0:T(8,128)}), f32[64,2048]{1,0:T(8,128)}) %reduce-scatter.10.cloned.1.call-update) | async-done | bytes 524304 | tf_op jit(solution)/shard_map/reduce_scatter | solution.py:81
  184.1 39.3 %reduce-scatter.8.cloned.1.call-done = f32[64,2048]{1,0:T(8,128)} async-done(((f32[512,2048]{1,0:T(8,128)}), f32[64,2048]{1,0:T(8,128)}) %reduce-scatter.8.cloned.1.call-update) | async-done | bytes 524304 | tf_op jit(solution)/shard_map/reduce_scatter | solution.py:80
  223.4 1.3 multiply_convert_fusion
  224.7 0.8 pad_maximum_fusion
  225.5 0.0 all-gather.5.cloned.1.call-update
  225.5 0.0 reduce-scatter.14.cloned.1.call-start
  225.5 28.6 %all-gather.5.cloned.1.call-done = bf16[512,2560]{1,0:T(8,128)(2,1)} async-done(((bf16[64,2560]{1,0:T(8,128)(2,1)}), bf16[512,2560]{1,0:T(8,128)(2,1)}) %all-gather.5.cloned.1.call-update) | async-done | bytes 2621456 | tf_op jit(solution)/shard_map/all_gather | solution.py:99
  254.2 5.1 %fusion = f32[512,1024]{1,0:T(8,128)S(1)} fusion(bf16[2048,1024]{1,0:T(8,128)(2,1)} %param.15, bf16[512,2560]{1,0:T(8,128)(2,1)} %all-gather.5.cloned.1.call-done), kind=kOutput, calls=%fused_computation | convolution fusion | flops 2147483648 | bytes 8388608 | tf_op jit(solution)/shard_map/dot_general | solution.py:100
  259.3 3.1 convolution_add_fusion
  262.5 72.7 %reduce-scatter.14.cloned.1.call-done = f32[32,1024]{1,0:T(8,128)} async-done(((f32[512,1024]{1,0:T(8,128)}), f32[32,1024]{1,0:T(8,128)}) %reduce-scatter.14.cloned.1.call-update) | async-done | bytes 131088 | tf_op jit(solution)/shard_map/reduce_scatter | solution.py:103
  335.2 1.5 fusion.14
  (34 shorter events, 0.3 us)
Async XLA Ops:
  7.2 154.3 %copy-start = (bf16[4,1024,256]{2,1,0:T(8,128)(2,1)S(1)}, bf16[4,1024,256]{2,1,0:T(8,128)(2,1)}, u32[]{:S(2)}) copy-start(bf16[4,1024,256]{2,1,0:T(8,128)(2,1)} %param.19) | copy-start | bytes 6291460
  7.2 73.1 %all-gather.3.cloned.1.call-start = ((), (), s32[]{:S(2)}) async-start(), calls=%async_computation.8 | async-start | bytes 1114112 | tf_op jit(solution)/shard_map/all_gather | solution.py:73
  40.1 71.3 %reduce-scatter.16.cloned.1.call-start = ((), (), s32[]{:S(2)}) async-start(), calls=%async_computation.14 | async-start | bytes 294912
  82.6 3.5 %copy-start.1 = (bf16[512,1024]{1,0:T(8,128)(2,1)S(1)}, bf16[512,1024]{1,0:T(8,128)(2,1)}, u32[]{:S(2)}) copy-start(bf16[512,1024]{1,0:T(8,128)(2,1)} %all-gather.3.cloned.1.call-done) | copy-start | bytes 3145732
  82.7 62.0 %reduce-scatter.12.cloned.1.call-start = ((), (), s32[]{:S(2)}) async-start(), calls=%async_computation.11 | async-start | bytes 1179648 | tf_op jit(solution)/shard_map/reduce_scatter | solution.py:82
  86.1 98.0 %reduce-scatter.10.cloned.1.call-start = ((), (), s32[]{:S(2)}) async-start(), calls=%async_computation.10 | async-start | bytes 4718592 | tf_op jit(solution)/shard_map/reduce_scatter | solution.py:81
  92.7 130.7 %reduce-scatter.8.cloned.1.call-start = ((), (), s32[]{:S(2)}) async-start(), calls=%async_computation.9 | async-start | bytes 4718592 | tf_op jit(solution)/shard_map/reduce_scatter | solution.py:80
  99.2 0.7 copy-start.6
  113.2 13.0 %all-to-all-start.1 = ((bf16[16,4,32]{2,1,0:T(4,128)(2,1)}), bf16[16,4,32]{2,1,0:T(4,128)(2,1)S(1)}, u32[]{:S(2)}, u32[]{:S(2)}) async-start(bf16[16,4,32]{2,1,0:T(4,128)(2,1)} %bitcast.5), calls=%async_computation.4 | async-start | bytes 32768 | tf_op jit(solution)/shard_map/all_to_all | solution.py:91
  126.3 36.1 %copy-start.4 = (bf16[4,512]{1,0:T(4,128)(2,1)}, bf16[4,512]{1,0:T(4,128)(2,1)S(1)}, u32[]{:S(2)}) copy-start(bf16[4,512]{1,0:T(4,128)(2,1)S(1)} %all_to_all.46) | copy-start | bytes 12292
  148.2 13.1 %all-to-all-start = ((bf16[16,4,512]{2,1,0:T(4,128)(2,1)}), bf16[16,4,512]{2,1,0:T(4,128)(2,1)S(1)}, u32[]{:S(2)}, u32[]{:S(2)}) async-start(bf16[16,4,512]{2,1,0:T(4,128)(2,1)} %all_to_all.40), calls=%async_computation.3 | async-start | bytes 131072 | tf_op jit(solution)/shard_map/all_to_all | solution.py:90
  154.8 99.4 %all-gather.5.cloned.1.call-start = ((), (), s32[]{:S(2)}) async-start(), calls=%async_computation.12 | async-start | bytes 2949120 | tf_op jit(solution)/shard_map/all_gather | solution.py:99
  161.4 1.6 copy-start.5
  225.5 33.8 %copy-start.3 = (bf16[512,1024]{1,0:T(8,128)(2,1)S(1)}, bf16[512,1024]{1,0:T(8,128)(2,1)}, u32[]{:S(2)}) copy-start(bf16[512,1024]{1,0:T(8,128)(2,1)} %param.18) | copy-start | bytes 3145732
  225.5 109.7 %reduce-scatter.14.cloned.1.call-start = ((), (), s32[]{:S(2)}) async-start(), calls=%async_computation.13 | async-start | bytes 2228224 | tf_op jit(solution)/shard_map/reduce_scatter | solution.py:103
  259.3 75.8 %copy-start.2 = (bf16[32,1024]{1,0:T(8,128)(2,1)S(1)}, bf16[32,1024]{1,0:T(8,128)(2,1)}, u32[]{:S(2)}) copy-start(bf16[32,1024]{1,0:T(8,128)(2,1)} %param.11) | copy-start | bytes 196612
Sparse Core Ops, SparseCore 0:
  40.2 40.0 all-gather.2
  82.8 28.5 reduce-scatter.15
  113.9 30.7 reduce-scatter.11
  147.1 36.9 reduce-scatter.9
  186.4 36.8 reduce-scatter.7
  225.6 28.5 all-gather.4
  262.6 72.5 reduce-scatter.13
where the time goes:
time: 345 us; the launch traced here: 344 us
  waiting for transfers between devices  234 us (68%)
  blocking collectives  38.5 us (11%)
  matrix products  28.4 us (8%)
  between operations  14.4 us (4%)
  starting transfers between devices  13.4 us (4%)
  other arithmetic  9.19 us (3%)
  local copies, waits for them, and re-layouts  5.59 us (2%)
    reduce_scatter x1, waiting for transfers between devices, local(): summed = lax.psum_scatter(terms, 'gy', scatter_dimension=0, tiled=True)  72.7 us
    all_gather x1, waiting for transfers between devices, local(): gathered = lax.all_gather(normed, 'gy', axis=0, tiled=True)  40.1 us
    reduce_scatter x1, waiting for transfers between devices, local(): lax.psum_scatter(gate_part, 'gx', scatter_dimension=0, tiled=True)  39.3 us
    all_gather x1, waiting for transfers between devices, local(): piece = lax.all_gather(joined, 'gx', axis=0, tiled=True)  28.6 us
    reduce_scatter x1, waiting for transfers between devices, local(): lax.psum_scatter(query_part, 'gx', scatter_dimension=0, tiled=True)  18.4 us
    psum x1, blocking collectives, local(): spread = lax.psum(jnp.sum(centered * centered, axis=1), 'gx') / width  14.7 us
    psum x1, blocking collectives, local(): mean = lax.psum(jnp.sum(values, axis=1), 'gx') / width  14.5 us
    unnamed x8, waiting for transfers between devices  11.3 us
  transfers between devices with their start and end apart: 9, of which 9 were waited for; matrix products, arithmetic and copies ran while one was open for 7% of the time, Pallas kernels for 0%

commit v1 on v0

v1 whole, which is shorter than its diff:
```python
import jax
import jax.numpy as jnp
import numpy as np
from jax import lax
from jax.experimental import pallas as pl
from jax.experimental.pallas import tpu as pltpu
from jax.sharding import PartitionSpec as P

EPS = 1e-05
MESH = pl.DeviceIdType.MESH
F32 = jnp.float32
BF16 = jnp.bfloat16
T = 4
ROWS = 512
WIDTH = 8192
DEPTH = 1024
HID = 2048
QC = 512
PAIR = 32
HEAD = 256
SLOTS = 1024
BLK = 32
PIECE = 128
OWN = 4


def iota(shape, dim):
    return lax.broadcasted_iota(jnp.int32, shape, dim)


def dot(a, b):
    return jnp.dot(a, b, preferred_element_type=F32)


def onehot(cond):
    return jnp.where(cond, 1.0, 0.0).astype(BF16)


def kernel(
    tokens, gain, lengths, freq, gate_h, up_h, down_h, query_h, pair_w, out_h, ck_h, cv_h,
    mixed, new_pair,
    gate_w, up_w, down_w, query_w, out_w, ck, cv, pair_p,
    st, xb, part, corecv, zs, zrecv, hid,
    qpart, qcore, qsum, qz, tab, ab, arecv, qall, npair, attk, bb, brecv, att,
    total, dpart, rs,
    lsem, st_s, st_r, tok_s, tok_r, core_s, core_r, z_s, z_r, agz_s, agz_r, agc_s, agc_r,
    qc_s, qc_r, qz_s, qz_r, a_s, a_r, b_s, b_r, attz_s, attz_r, attc_s, attc_r, rs_s, rs_r,
):
    i = lax.axis_index("gx")
    j = lax.axis_index("gy")
    z, c = i // 2, i % 2
    y, x = j // 4, j % 4
    sib = (i + 1 - 2 * c, j)
    pending = []

    def zdev(k):
        return (((z + k) % 4) * 2 + c, j)

    def send(src, dst, ss, rr, dev):
        cp = pltpu.make_async_remote_copy(
            src_ref=src, dst_ref=dst, send_sem=ss, recv_sem=rr, device_id=dev, device_id_type=MESH
        )
        cp.start()
        pending.append(cp)
        return cp

    loads = {}
    for n, (name, src, dst) in enumerate(
        [
            ("gate", gate_h, gate_w), ("up", up_h, up_w), ("query", query_h, query_w),
            ("ck", ck_h, ck), ("cv", cv_h, cv), ("down", down_h, down_w), ("out", out_h, out_w),
        ]
    ):
        loads[name] = pltpu.make_async_copy(src, dst, lsem.at[n])
        loads[name].start()

    barrier = pltpu.get_barrier_semaphore()
    for k in range(1, 8):
        pl.semaphore_signal(barrier, inc=1, device_id=((i + k) % 8, j), device_id_type=MESH)
    for k in range(1, 16):
        pl.semaphore_signal(barrier, inc=1, device_id=(i, (j + k) % 16), device_id_type=MESH)

    values = tokens[...].astype(F32)
    mean_l = jnp.sum(values, axis=1, keepdims=True) * (1.0 / DEPTH)
    off = values - mean_l
    dev_l = jnp.sum(off * off, axis=1, keepdims=True)
    diag = iota((BLK, 128), 0) == iota((BLK, 128), 1)

    def to_row(col):
        return jnp.sum(jnp.where(diag, col, 0.0), axis=0, keepdims=True)

    def to_col(row):
        return jnp.sum(jnp.where(diag, row, 0.0), axis=1, keepdims=True)

    sub = iota((8, 128), 0)
    st[0] = jnp.where(sub == 0, to_row(mean_l), jnp.where(sub == 1, to_row(dev_l), 0.0))
    pl.semaphore_wait(barrier, 22)

    cps = []
    for k in range(1, 8):
        cps.append(send(st.at[0], st.at[k], st_s.at[k], st_r.at[k], ((i + k) % 8, j)))

    place = onehot(iota((PAIR, 128), 1) == iota((PAIR, 128), 0) + PAIR * (j % 4))
    pair_p[...] = dot(pair_w[...], place).astype(BF16)

    for cp in cps:
        cp.wait_recv()
    means = [st[k, 0:1, :] for k in range(8)]
    mean = means[0]
    for k in range(1, 8):
        mean = mean + means[k]
    mean = mean * 0.125
    spread = jnp.zeros_like(mean)
    for k in range(8):
        gap = means[k] - mean
        spread = spread + (st[k, 1:2, :] + DEPTH * (gap * gap))
    scale = lax.rsqrt(spread * (1.0 / WIDTH) + EPS)
    xb[0] = ((values - to_col(mean)) * to_col(scale) * gain[...]).astype(BF16)

    toks = {}
    for t in range(T):
        for dy in range(4):
            dx = (t - dy) % 4
            if dx == 0 and dy == 0:
                continue
            dst = (i, ((y + 4 - dy) % 4) * 4 + (x + 4 - dx) % 4)
            b = 4 * t + dy
            toks[b] = send(xb.at[0], xb.at[b], tok_s.at[b], tok_r.at[b], dst)

    lens = jnp.zeros((64, 128), jnp.int32)
    row64 = iota((64, 128), 0)
    for r in range(64):
        lens = jnp.where(row64 == r, lengths[r], lens)
    lens = lens[:, 0:1].astype(F32)
    angle = lens * freq[...]
    tab[0] = jnp.cos(angle)
    tab[1] = jnp.sin(angle)

    def wait_tokens(t):
        for dy in range(4):
            if 4 * t + dy in toks:
                toks[4 * t + dy].wait_recv()

    def piece_rows(t):
        return xb[4 * t : 4 * t + 4].reshape(PIECE, DEPTH)

    core = {}

    def gate_up(t):
        def body(d, carry):
            rows = piece_rows(t)
            cols = pl.ds(pl.multiple_of(d * 256, 256), 256)
            g = dot(rows, gate_w[:, cols])
            u = dot(rows, up_w[:, cols])
            part[t, d % 2, d // 2, :, 0:256] = g.astype(BF16)
            part[t, d % 2, d // 2, :, 256:512] = u.astype(BF16)
            return carry

        lax.fori_loop(0, 8, body, 0)
        core[t] = send(part.at[t, 1 - c], corecv.at[t], core_s.at[t], core_r.at[t], sib)

    zcp = {}

    def core_add(t):
        core[t].wait_recv()

        def body(k, carry):
            zs[t, k] = (part[t, c, k].astype(F32) + corecv[t, k].astype(F32)).astype(BF16)
            return carry

        lax.fori_loop(0, 4, body, 0)
        for k in (1, 3, 2):
            zcp[t, k] = send(
                zs.at[t, (z + k) % 4], zrecv.at[t, k - 1], z_s.at[t, k - 1], z_r.at[t, k - 1], zdev(k)
            )

    agz, agc = {}, {}

    def hidden_cols(k):
        owner = ((z + 4 - k) % 4) * 2 + c
        return pl.ds(pl.multiple_of(owner * 256, 256), 256)

    def finish_hidden(t):
        for k in (1, 2, 3):
            zcp[t, k].wait_recv()
        both = part[t, c, z].astype(F32) + corecv[t, z].astype(F32)
        for k in range(3):
            both = both + zrecv[t, k].astype(F32)
        g, u = both[:, 0:256], both[:, 256:512]
        h = (g / (1.0 + jnp.exp(-g)) * u).astype(BF16)
        mine = hidden_cols(0)
        hid[t, :, mine] = h
        block = hid.at[t, :, mine]
        for k in (1, 3, 2):
            agz[t, k] = send(block, block, agz_s.at[t, k - 1], agz_r.at[t, k - 1], zdev(k))
        agc[t, 0] = send(block, block, agc_s.at[t, 0], agc_r.at[t, 0], sib)

    def forward_hidden(t):
        for k in (1, 3, 2):
            agz[t, k].wait_recv()
            block = hid.at[t, :, hidden_cols(k)]
            agc[t, k] = send(block, block, agc_s.at[t, k], agc_r.at[t, k], sib)

    def down(t):
        for k in range(4):
            agc[t, k].wait_recv()

        def body(n, carry):
            cols = pl.ds(pl.multiple_of(n * 512, 512), 512)
            total[t, :, cols] = dot(hid[t], down_w[:, cols])
            return carry

        lax.fori_loop(0, 2, body, 0)

    qcp = {}

    def query_product():
        for t in range(T):
            rows = piece_rows(t)
            q = dot(rows, query_w[...])
            p = dot(rows, pair_p[...])
            for dy in range(4):
                zz = (y + dy) % 4
                xx = (x + (t - dy) % 4) % 4
                piece = slice(BLK * dy, BLK * dy + BLK)
                qpart[xx // 2, zz, xx % 2, :, 0:QC] = q[piece]
                qpart[xx // 2, zz, xx % 2, :, QC:] = p[piece]
        qcp["core"] = send(qpart.at[1 - c], qcore, qc_s.at[0], qc_r.at[0], sib)

    def query_core_add():
        qcp["core"].wait_recv()

        def body(k, carry):
            qsum[k] = qpart[c, k] + qcore[k]
            return carry

        lax.fori_loop(0, 4, body, 0)
        for k in (1, 3, 2):
            qcp[k] = send(
                qsum.at[(z + k) % 4], qz.at[k - 1], qz_s.at[k - 1], qz_r.at[k - 1], zdev(k)
            )

    def spread_matrix(h):
        out = iota((128, 64), 0)
        return onehot(
            (((out >> 2) & 1) == h) & (iota((128, 64), 1) == (out >> 3) * 4 + (out & 3))
        )

    def turn(v, cosine, sine):
        width = v.shape[1]
        even = (iota(v.shape, 1) & 1) == 0
        swap = jnp.where(even, pltpu.roll(v, width - 1, 1), pltpu.roll(v, 1, 1))
        return v * cosine + swap * jnp.where(even, -sine, sine)

    acp = {}

    def query_finish():
        for k in (1, 2, 3):
            qcp[k].wait_recv()
        full = qsum[z]
        for k in range(3):
            full = full + qz[k]
        full = full.reshape(64, QC + 128)
        cosine, sine = tab[0], tab[1]
        q0 = turn(full[:, 0:256], cosine, sine).astype(BF16)
        q1 = turn(full[:, 256:512], cosine, sine).astype(BF16)
        group = j // 4
        low, is_key = group == 0, group < 2
        pc = jnp.where(is_key, jnp.where(low, cosine[:, 0:128], cosine[:, 128:256]), 1.0)
        ps = jnp.where(is_key, jnp.where(low, sine[:, 0:128], sine[:, 128:256]), 0.0)
        pr = turn(full[:, QC:], pc, ps).astype(BF16)
        m0, m1 = spread_matrix(0), spread_matrix(1)
        ab[:, :, 0:256] = (dot(m0, q0) + dot(m1, q1)).reshape(16, 8, 256)
        ab[:, :, 256:384] = dot(m0, pr).reshape(16, 8, 128)
        for k in range(1, 16):
            to = (j + k) % 16
            acp[k] = send(ab.at[to], arecv.at[j], a_s.at[k], a_r.at[k], (i, to))
        arecv[j] = ab[j]

    bcp = {}

    def attention():
        for k in range(1, 16):
            acp[k].wait_recv()
        queries = arecv[:, :, 0:256].reshape(128, 256).astype(BF16)
        out = iota((128, 128), 0)
        inn = iota((128, 128), 1)
        order = onehot(
            ((out >> 5) == (inn & 3)) & (((out >> 1) & 15) == (inn >> 3)) & ((out & 1) == ((inn >> 2) & 1))
        )
        qall[...] = dot(order, queries).astype(BF16).reshape(OWN, 32, HEAD)
        for g in range(4):
            cols = arecv[4 * g, :, 256:384]
            for s in range(1, 4):
                cols = cols + arecv[4 * g + s, :, 256:384]
            npair[:, 128 * g : 128 * g + 128] = cols
        new_pair[...] = npair[0:OWN, :].astype(BF16)

        def body(k, carry):
            q = qall[k]
            s = lax.dot_general(
                q, ck[k], (((1,), (1,)), ((), ())), preferred_element_type=F32
            ) * (HEAD ** -0.5)
            pair = npair[pl.ds(k, 1), :]
            fresh = jnp.sum(q.astype(F32) * pair[:, 0:HEAD], axis=1, keepdims=True) * (HEAD ** -0.5)
            valid = iota((32, SLOTS), 1) < lengths[OWN * j + k]
            top = jnp.maximum(jnp.max(jnp.where(valid, s, -1e30), axis=1, keepdims=True), fresh)
            w = jnp.where(valid, jnp.exp(s - top), 0.0)
            fw = jnp.exp(fresh - top)
            tot = jnp.sum(w, axis=1, keepdims=True) + fw
            probs = (w / tot).astype(BF16)
            fp = (fw / tot).astype(BF16).astype(F32)
            attk[k] = (dot(probs, cv[k]) + fp * pair[:, HEAD:]).astype(BF16)
            return carry

        lax.fori_loop(0, OWN, body, 0)
        back = onehot(
            ((inn >> 5) == (out & 3)) & (((inn >> 1) & 15) == (out >> 3)) & ((inn & 1) == ((out >> 2) & 1))
        )
        bb[...] = dot(back, attk[...].reshape(128, HEAD)).reshape(16, 8, HEAD)
        for k in range(1, 16):
            to = (j + k) % 16
            bcp[k] = send(bb.at[to], brecv.at[j], b_s.at[k], b_r.at[k], (i, to))
        brecv[j] = bb[j]

    attz, attc = {}, {}

    def attended_spread():
        for k in range(1, 16):
            bcp[k].wait_recv()
        rows = brecv[...].reshape(128, HEAD).astype(BF16)
        inn = iota((64, 128), 1)
        for h in (0, 1):
            gather = onehot(
                (((inn >> 2) & 1) == h) & (iota((64, 128), 0) == (inn >> 3) * 4 + (inn & 3))
            )
            att[i, :, HEAD * h : HEAD * h + HEAD] = dot(gather, rows).astype(BF16)
        for k in (1, 3, 2):
            attz[k] = send(att.at[i], att.at[i], attz_s.at[k - 1], attz_r.at[k - 1], zdev(k))
        attc[0] = send(att.at[i], att.at[i], attc_s.at[0], attc_r.at[0], sib)

    def attended_forward():
        for k in (1, 3, 2):
            attz[k].wait_recv()
            block = att.at[((z + 4 - k) % 4) * 2 + c]
            attc[k] = send(block, block, attc_s.at[k], attc_r.at[k], sib)

    rcp = {}

    def out_product(t):
        blocks = []
        for dy in range(4):
            xx = (x + (t - dy) % 4) % 4
            start = pl.multiple_of((xx % 2) * BLK, BLK)
            blocks.append(att[2 * ((y + dy) % 4) + xx // 2, pl.ds(start, BLK), :])
        rows = jnp.concatenate(blocks, axis=0)
        for n in range(2):
            cols = slice(512 * n, 512 * n + 512)
            v = total[t, :, cols] + dot(rows, out_w[:, cols])
            dpart[t, :, :, cols] = v.astype(BF16).reshape(4, BLK, 512)
        for dy in range(4):
            dx = (t - dy) % 4
            if dx == 0 and dy == 0:
                continue
            b = 4 * t + dy
            dst = (i, ((y + dy) % 4) * 4 + (x + dx) % 4)
            rcp[b] = send(dpart.at[t, dy], rs.at[b], rs_s.at[b], rs_r.at[b], dst)

    loads["gate"].wait()
    loads["up"].wait()
    wait_tokens(0)
    gate_up(0)
    wait_tokens(1)
    gate_up(1)
    core_add(0)
    wait_tokens(2)
    wait_tokens(3)
    loads["query"].wait()
    query_product()
    core_add(1)
    gate_up(2)
    query_core_add()
    finish_hidden(0)
    core_add(2)
    gate_up(3)
    query_finish()
    forward_hidden(0)
    core_add(3)
    finish_hidden(1)
    loads["ck"].wait()
    loads["cv"].wait()
    attention()
    forward_hidden(1)
    loads["down"].wait()
    down(0)
    finish_hidden(2)
    attended_spread()
    forward_hidden(2)
    down(1)
    finish_hidden(3)
    attended_forward()
    down(2)
    forward_hidden(3)
    loads["out"].wait()
    for k in range(4):
        attc[k].wait_recv()
    out_product(0)
    out_product(1)
    out_product(2)
    down(3)
    out_product(3)

    result = tokens[...].astype(F32) + dpart[0, 0].astype(F32)
    for b in range(1, 16):
        rcp[b].wait_recv()
        result = result + rs[b].astype(F32)
    mixed[...] = result.astype(BF16)
    for cp in pending:
        cp.wait_send()


def local(
    tokens, gain, gate_weight, up_weight, down_weight, query_weight, pair_weight, out_weight,
    cache_k, cache_v, lengths,
):
    freq = np.power(10000.0, -2.0 * (np.arange(HEAD) // 2) / HEAD).astype(np.float32)[None, :]
    vm = pl.BlockSpec(memory_space=pltpu.VMEM)
    sm = pl.BlockSpec(memory_space=pltpu.SMEM)
    hb = pl.BlockSpec(memory_space=pl.ANY)
    dma = pltpu.SemaphoreType.DMA
    v = pltpu.VMEM
    return pl.pallas_call(
        kernel,
        out_shape=(
            jax.ShapeDtypeStruct((BLK, DEPTH), BF16),
            jax.ShapeDtypeStruct((OWN, 2 * HEAD), BF16),
        ),
        in_specs=[vm, vm, sm, vm, hb, hb, hb, hb, vm, hb, hb, hb],
        out_specs=(vm, vm),
        scratch_shapes=[
            v((DEPTH, HID), BF16), v((DEPTH, HID), BF16), v((HID, DEPTH), BF16),
            v((DEPTH, QC), BF16), v((QC, DEPTH), BF16),
            v((OWN, SLOTS, HEAD), BF16), v((OWN, SLOTS, HEAD), BF16), v((DEPTH, 128), BF16),
            v((8, 8, 128), F32), v((16, BLK, DEPTH), BF16),
            v((T, 2, 4, PIECE, 512), BF16), v((T, 4, PIECE, 512), BF16),
            v((T, 4, PIECE, 512), BF16), v((T, 3, PIECE, 512), BF16), v((T, PIECE, HID), BF16),
            v((2, 4, 2, BLK, QC + 128), F32), v((4, 2, BLK, QC + 128), F32),
            v((4, 2, BLK, QC + 128), F32), v((3, 2, BLK, QC + 128), F32),
            v((2, 64, HEAD), F32), v((16, 8, 384), F32), v((16, 8, 384), F32),
            v((OWN, 32, HEAD), BF16), v((8, 2 * HEAD), F32), v((OWN, 32, HEAD), BF16),
            v((16, 8, HEAD), F32), v((16, 8, HEAD), F32), v((8, 64, QC), BF16),
            v((T, PIECE, DEPTH), F32), v((T, 4, BLK, DEPTH), BF16), v((16, BLK, DEPTH), BF16),
            dma((7,)), dma((8,)), dma((8,)), dma((16,)), dma((16,)), dma((T,)), dma((T,)),
            dma((T, 3)), dma((T, 3)), dma((T, 3)), dma((T, 3)), dma((T, 4)), dma((T, 4)),
            dma((1,)), dma((1,)), dma((3,)), dma((3,)), dma((16,)), dma((16,)),
            dma((16,)), dma((16,)), dma((3,)), dma((3,)), dma((4,)), dma((4,)),
            dma((16,)), dma((16,)),
        ],
        compiler_params=pltpu.CompilerParams(
            collective_id=0, has_side_effects=True, vmem_limit_bytes=56 * 1024 * 1024
        ),
        cost_estimate=pl.CostEstimate(
            flops=2 * ROWS * DEPTH * 7200, bytes_accessed=20 * 1024 * 1024, transcendentals=1 << 20
        ),
        name="layer",
    )(
        tokens, gain.reshape(1, DEPTH), lengths, jnp.asarray(freq), gate_weight, up_weight,
        down_weight, query_weight, pair_weight, out_weight, cache_k, cache_v,
    )


def solution(mesh):
    in_specs = (
        P("gy", "gx"),
        P("gx"),
        P("gx", "gy"),
        P("gx", "gy"),
        P("gy", "gx"),
        P("gx", "gy"),
        P("gx", "gy"),
        P("gy", "gx"),
        P(("gx", "gy"), None, None),
        P(("gx", "gy"), None, None),
        P("gx"),
    )
    out_specs = (P("gy", "gx"), P(("gx", "gy"), None))
    return jax.shard_map(local, mesh=mesh, in_specs=in_specs, out_specs=out_specs, check_vma=False)
```

time: 345 us -> 97.3 us (0.28)
  waiting for transfers between devices: 234 us -> 0 us
  Pallas kernels: 0 us -> 90.3 us
  blocking collectives: 38.5 us -> 0 us
  matrix products: 28.4 us -> 0 us
  between operations: 14.4 us -> 0.64 us
  starting transfers between devices: 13.4 us -> 0 us
  other arithmetic: 9.19 us -> 0 us
    reduce_scatter x4 -> x0, waiting for transfers between devices: 141 us -> none  [the longest x1 72.7 us: local(): summed = lax.psum_scatter(terms, 'gy', scatter_dimension=0, tiled=True)]
    pallas_call x0 -> x1, Pallas kernels: none -> 90.3 us  [local(): pl.pallas_call(kernel, out_shape=(jax.ShapeDtypeStruct((BLK, DEPTH), BF16...]
    all_gather x2 -> x0, waiting for transfers between devices: 68.8 us -> none  [the longest x1 40.1 us: local(): gathered = lax.all_gather(normed, 'gy', axis=0, tiled=True)]
    psum x2 -> x0, blocking collectives: 29.2 us -> none  [the longest x1 14.7 us: local(): spread = lax.psum(jnp.sum(centered * centered, axis=1), 'gx') / width]
    dot_general x8 -> x0, matrix products: 26.1 us -> none  [the longest x1 6.5 us: local(): jnp.dot(gathered, gate_weight, preferred_element_type=jnp.float32)]
    all_to_all x2 -> x0, starting transfers between devices: 13.1 us -> none  [the longest x1 6.55 us: local(): lax.all_to_all(query_turned, 'gy', split_axis=0, concat_axis=1, tiled=True)]
    all_to_all x2 -> x0, waiting for transfers between devices: 12.6 us -> none  [the longest x1 6.46 us: local(): lax.all_to_all(query_turned, 'gy', split_axis=0, concat_axis=1, tiled=True)]
    unnamed x8 -> x0, waiting for transfers between devices: 11.3 us -> none
  transfers between devices with their start and end apart: 9 -> 0, of which waited for: 9 -> 0; matrix products, arithmetic and copies ran while one was open for 7% -> 0% of each run, Pallas kernels for 0% -> 0%
where the time goes in v1:
time: 97.3 us; the launch traced here: 95.4 us
  Pallas kernels  90.3 us (93%)
  local copies, waits for them, and re-layouts  4.42 us (5%)
    pallas_call x1, Pallas kernels, local(): pl.pallas_call(kernel, out_shape=(jax.ShapeDtypeStruct((BLK, DEPTH), BF16...  90.3 us
    unnamed x3, local copies, waits for them, and re-layouts  4.42 us

profile of v1, /device:TPU:1, one launch (start us, length us, event | category | flops | bytes accessed | tf_op | source)
XLA Modules:
  0.0 95.4 jit_solution(5434259127205300153)
XLA Ops:
  0.6 1.7 %copy.14.pair_w = bf16[1024,32]{1,0:T(8,128)(2,1)} copy(bf16[1024,32]{0,1:T(8,128)(2,1)} %param.18) | data formatting | bytes 131072 | tf_op args[6]
  2.3 90.3 %layer.1 = (bf16[32,1024]{1,0:T(8,128)(2,1)}, bf16[4,512]{1,0:T(4,128)(2,1)}) custom-call(bf16[32,1024]{1,0:T(8,128)(2,1)} %tokens.1, f32[1,1024]{1,0:T(1,128)} %bitcast.1, s32[64]{0:T(128)} %lengths.1, f32[1,256]{1,0:T(1,128)} %constant.2.clone.freq, bf16[1024,2048]{1,0:T(8,128)(2,1)} %gate_h.1, bf16[1024,2048]{1,0:T(8,128)(2,1)} %up_h.1, ...), custom_call_target="tpu_custom_call" | custom-call | flops 7549747200 | bytes 20971520 | tf_op jit(solution)/shard_map/layer/pallas_call | solution.py:432
  92.6 1.5 %copy.17 = bf16[32,1024]{1,0:T(8,128)(2,1)} copy(bf16[32,1024]{1,0:T(8,128)(2,1)} %get-tuple-element.4) | data formatting | bytes 131072
  94.1 1.3 %copy.18 = bf16[4,512]{1,0:T(4,128)(2,1)} copy(bf16[4,512]{1,0:T(4,128)(2,1)} %get-tuple-element.5) | data formatting | bytes 8192

commit v2 on v1

--- a/solution.py
+++ b/solution.py
@@ -37,11 +37,12 @@
 
 
 def kernel(
-    tokens, gain, lengths, freq, gate_h, up_h, down_h, query_h, pair_w, out_h, ck_h, cv_h,
+    tokens_h, gain_h, lengths, freq_h, gate_h, up_h, down_h, query_h, pair_h, out_h, ck_h, cv_h,
     mixed, new_pair,
+    tokens, gain, freq, pair_w,
     gate_w, up_w, down_w, query_w, out_w, ck, cv, pair_p,
-    st, xb, part, corecv, zs, zrecv, hid,
-    qpart, qcore, qsum, qz, tab, ab, arecv, qall, npair, attk, bb, brecv, att,
+    st, xb, part, corecv, zs, zsum, zrecv, hid,
+    qpart, qcore, qsum, qfwd, qz, tab, ab, arecv, qall, npair, attk, bb, brecv, att,
     total, dpart, rs,
     lsem, st_s, st_r, tok_s, tok_r, core_s, core_r, z_s, z_r, agz_s, agz_r, agc_s, agc_r,
     qc_s, qc_r, qz_s, qz_r, a_s, a_r, b_s, b_r, attz_s, attz_r, attc_s, attc_r, rs_s, rs_r,
@@ -67,7 +68,8 @@
     loads = {}
     for n, (name, src, dst) in enumerate(
         [
-            ("gate", gate_h, gate_w), ("up", up_h, up_w), ("query", query_h, query_w),
+            ("tokens", tokens_h, tokens), ("pair", pair_h, pair_w), ("gain", gain_h, gain),
+            ("freq", freq_h, freq), ("gate", gate_h, gate_w), ("up", up_h, up_w), ("query", query_h, query_w),
             ("ck", ck_h, ck), ("cv", cv_h, cv), ("down", down_h, down_w), ("out", out_h, out_w),
         ]
     ):
@@ -80,6 +82,7 @@
     for k in range(1, 16):
         pl.semaphore_signal(barrier, inc=1, device_id=(i, (j + k) % 16), device_id_type=MESH)
 
+    loads["tokens"].wait()
     values = tokens[...].astype(F32)
     mean_l = jnp.sum(values, axis=1, keepdims=True) * (1.0 / DEPTH)
     off = values - mean_l
@@ -101,7 +104,12 @@
         cps.append(send(st.at[0], st.at[k], st_s.at[k], st_r.at[k], ((i + k) % 8, j)))
 
     place = onehot(iota((PAIR, 128), 1) == iota((PAIR, 128), 0) + PAIR * (j % 4))
-    pair_p[...] = dot(pair_w[...], place).astype(BF16)
+    loads["pair"].wait()
+    pair_p[...] = lax.dot_general(
+        pair_w[...], place, (((0,), (0,)), ((), ())), preferred_element_type=F32
+    ).astype(BF16)
+    loads["gain"].wait()
+    loads["freq"].wait()
 
     for cp in cps:
         cp.wait_recv()
@@ -147,31 +155,51 @@
     core = {}
 
     def gate_up(t):
-        def body(d, carry):
-            rows = piece_rows(t)
-            cols = pl.ds(pl.multiple_of(d * 256, 256), 256)
-            g = dot(rows, gate_w[:, cols])
-            u = dot(rows, up_w[:, cols])
-            part[t, d % 2, d // 2, :, 0:256] = g.astype(BF16)
-            part[t, d % 2, d // 2, :, 256:512] = u.astype(BF16)
-            return carry
-
-        lax.fori_loop(0, 8, body, 0)
+        def half(cc):
+            def body(k, carry):
+                rows = piece_rows(t)
+                cols = pl.ds(pl.multiple_of((2 * k + cc) * 256, 256), 256)
+                g = dot(rows, gate_w[:, cols])
+                u = dot(rows, up_w[:, cols])
+                part[t, cc, k, :, 0:256] = g.astype(BF16)
+                part[t, cc, k, :, 256:512] = u.astype(BF16)
+                return carry
+
+            lax.fori_loop(0, 4, body, 0)
+
+        half(1 - c)
         core[t] = send(part.at[t, 1 - c], corecv.at[t], core_s.at[t], core_r.at[t], sib)
+        half(c)
 
     zcp = {}
+
+    up_dev, dn_dev = zdev(1), zdev(3)
+    far, nxt, prv = (z + 2) % 4, (z + 1) % 4, (z + 3) % 4
+    lo, hi = slice(0, 64), slice(64, 128)
 
     def core_add(t):
         core[t].wait_recv()
 
-        def body(k, carry):
+        def both(k):
             zs[t, k] = (part[t, c, k].astype(F32) + corecv[t, k].astype(F32)).astype(BF16)
-            return carry
-
-        lax.fori_loop(0, 4, body, 0)
-        for k in (1, 3, 2):
-            zcp[t, k] = send(
-                zs.at[t, (z + k) % 4], zrecv.at[t, k - 1], z_s.at[t, k - 1], z_r.at[t, k - 1], zdev(k)
+
+        def go(n, src, dev):
+            zcp[t, n] = send(src, zrecv.at[t, n], z_s.at[t, n], z_r.at[t, n], dev)
+
+        both(far)
+        go(0, zs.at[t, far, lo], up_dev)
+        go(1, zs.at[t, far, hi], dn_dev)
+        both(nxt)
+        go(2, zs.at[t, nxt, hi], up_dev)
+        both(prv)
+        go(3, zs.at[t, prv, lo], dn_dev)
+
+    def pass_on(t):
+        for n, (to, half, dev) in enumerate(((nxt, lo, up_dev), (prv, hi, dn_dev))):
+            zcp[t, n].wait_recv()
+            zsum[t, n] = (zs[t, to, half].astype(F32) + zrecv[t, n].astype(F32)).astype(BF16)
+            zcp[t, 4 + n] = send(
+                zsum.at[t, n], zrecv.at[t, 4 + n], z_s.at[t, 4 + n], z_r.at[t, 4 + n], dev
             )
 
     agz, agc = {}, {}
@@ -181,25 +209,33 @@
         return pl.ds(pl.multiple_of(owner * 256, 256), 256)
 
     def finish_hidden(t):
-        for k in (1, 2, 3):
-            zcp[t, k].wait_recv()
-        both = part[t, c, z].astype(F32) + corecv[t, z].astype(F32)
-        for k in range(3):
-            both = both + zrecv[t, k].astype(F32)
-        g, u = both[:, 0:256], both[:, 256:512]
-        h = (g / (1.0 + jnp.exp(-g)) * u).astype(BF16)
+        for n in (3, 2, 4, 5):
+            zcp[t, n].wait_recv()
         mine = hidden_cols(0)
-        hid[t, :, mine] = h
+        for half, n, m in ((lo, 4, 3), (hi, 2, 5)):
+            v = part[t, c, z, half].astype(F32) + corecv[t, z, half].astype(F32)
+            v = v + (zrecv[t, n].astype(F32) + zrecv[t, m].astype(F32))
+            g, u = v[:, 0:256], v[:, 256:512]
+            hid[t, half, mine] = (g / (1.0 + jnp.exp(-g)) * u).astype(BF16)
         block = hid.at[t, :, mine]
-        for k in (1, 3, 2):
-            agz[t, k] = send(block, block, agz_s.at[t, k - 1], agz_r.at[t, k - 1], zdev(k))
+        agz[t, 0] = send(block, block, agz_s.at[t, 0], agz_r.at[t, 0], up_dev)
+        agz[t, 1] = send(block, block, agz_s.at[t, 1], agz_r.at[t, 1], dn_dev)
         agc[t, 0] = send(block, block, agc_s.at[t, 0], agc_r.at[t, 0], sib)
 
     def forward_hidden(t):
-        for k in (1, 3, 2):
-            agz[t, k].wait_recv()
+        for n, (k, half, dev) in enumerate(((1, lo, up_dev), (3, hi, dn_dev))):
+            agz[t, n].wait_recv()
+            part_of = hid.at[t, half, hidden_cols(k)]
+            agz[t, 2 + n] = send(part_of, part_of, agz_s.at[t, 2 + n], agz_r.at[t, 2 + n], dev)
+        for n, k in ((1, 1), (2, 3)):
             block = hid.at[t, :, hidden_cols(k)]
-            agc[t, k] = send(block, block, agc_s.at[t, k], agc_r.at[t, k], sib)
+            agc[t, n] = send(block, block, agc_s.at[t, n], agc_r.at[t, n], sib)
+
+    def forward_far(t):
+        agz[t, 2].wait_recv()
+        agz[t, 3].wait_recv()
+        block = hid.at[t, :, hidden_cols(2)]
+        agc[t, 3] = send(block, block, agc_s.at[t, 3], agc_r.at[t, 3], sib)
 
     def down(t):
         for k in range(4):
@@ -230,15 +266,22 @@
     def query_core_add():
         qcp["core"].wait_recv()
 
-        def body(k, carry):
-            qsum[k] = qpart[c, k] + qcore[k]
-            return carry
-
-        lax.fori_loop(0, 4, body, 0)
-        for k in (1, 3, 2):
-            qcp[k] = send(
-                qsum.at[(z + k) % 4], qz.at[k - 1], qz_s.at[k - 1], qz_r.at[k - 1], zdev(k)
-            )
+        def go(n, src, dev):
+            qcp[n] = send(src, qz.at[n], qz_s.at[n], qz_r.at[n], dev)
+
+        qsum[far] = qpart[c, far] + qcore[far]
+        go(0, qsum.at[far, 0], up_dev)
+        go(1, qsum.at[far, 1], dn_dev)
+        qsum[nxt] = qpart[c, nxt] + qcore[nxt]
+        go(2, qsum.at[nxt, 1], up_dev)
+        qsum[prv] = qpart[c, prv] + qcore[prv]
+        go(3, qsum.at[prv, 0], dn_dev)
+
+    def query_pass_on():
+        for n, (to, half, dev) in enumerate(((nxt, 0, up_dev), (prv, 1, dn_dev))):
+            qcp[n].wait_recv()
+            qfwd[n] = qsum[to, half] + qz[n]
+            qcp[4 + n] = send(qfwd.at[n], qz.at[4 + n], qz_s.at[4 + n], qz_r.at[4 + n], dev)
 
     def spread_matrix(h):
         out = iota((128, 64), 0)
@@ -255,12 +298,15 @@
     acp = {}
 
     def query_finish():
-        for k in (1, 2, 3):
-            qcp[k].wait_recv()
-        full = qsum[z]
-        for k in range(3):
-            full = full + qz[k]
-        full = full.reshape(64, QC + 128)
+        for n in (3, 2, 4, 5):
+            qcp[n].wait_recv()
+        full = jnp.concatenate(
+            [
+                qpart[c, z, 0] + qcore[z, 0] + (qz[4] + qz[3]),
+                qpart[c, z, 1] + qcore[z, 1] + (qz[2] + qz[5]),
+            ],
+            axis=0,
+        )
         cosine, sine = tab[0], tab[1]
         q0 = turn(full[:, 0:256], cosine, sine).astype(BF16)
         q1 = turn(full[:, 256:512], cosine, sine).astype(BF16)
@@ -335,17 +381,33 @@
                 (((inn >> 2) & 1) == h) & (iota((64, 128), 0) == (inn >> 3) * 4 + (inn & 3))
             )
             att[i, :, HEAD * h : HEAD * h + HEAD] = dot(gather, rows).astype(BF16)
-        for k in (1, 3, 2):
-            attz[k] = send(att.at[i], att.at[i], attz_s.at[k - 1], attz_r.at[k - 1], zdev(k))
-        attc[0] = send(att.at[i], att.at[i], attc_s.at[0], attc_r.at[0], sib)
+        block = att.at[i]
+        attz[0] = send(block, block, attz_s.at[0], attz_r.at[0], up_dev)
+        attz[1] = send(block, block, attz_s.at[1], attz_r.at[1], dn_dev)
+        attc[0] = send(block, block, attc_s.at[0], attc_r.at[0], sib)
 
     def attended_forward():
-        for k in (1, 3, 2):
-            attz[k].wait_recv()
+        for n, (k, half, dev) in enumerate(
+            ((1, slice(0, 32), up_dev), (3, slice(32, 64), dn_dev))
+        ):
+            attz[n].wait_recv()
+            part_of = att.at[((z + 4 - k) % 4) * 2 + c, half]
+            attz[2 + n] = send(part_of, part_of, attz_s.at[2 + n], attz_r.at[2 + n], dev)
+        for n, k in ((1, 1), (2, 3)):
             block = att.at[((z + 4 - k) % 4) * 2 + c]
-            attc[k] = send(block, block, attc_s.at[k], attc_r.at[k], sib)
+            attc[n] = send(block, block, attc_s.at[n], attc_r.at[n], sib)
+
+    def attended_far():
+        attz[2].wait_recv()
+        attz[3].wait_recv()
+        block = att.at[far * 2 + c]
+        attc[3] = send(block, block, attc_s.at[3], attc_r.at[3], sib)
 
     rcp = {}
+
+    def wait_attended():
+        for k in range(4):
+            attc[k].wait_recv()
 
     def out_product(t):
         blocks = []
@@ -370,43 +432,52 @@
     loads["up"].wait()
     wait_tokens(0)
     gate_up(0)
+    core_add(0)
     wait_tokens(1)
     gate_up(1)
-    core_add(0)
+    core_add(1)
+    pass_on(0)
     wait_tokens(2)
     wait_tokens(3)
     loads["query"].wait()
     query_product()
-    core_add(1)
-    gate_up(2)
+    pass_on(1)
     query_core_add()
     finish_hidden(0)
+    gate_up(2)
+    query_pass_on()
     core_add(2)
+    forward_hidden(0)
+    finish_hidden(1)
     gate_up(3)
     query_finish()
-    forward_hidden(0)
+    pass_on(2)
+    forward_far(0)
     core_add(3)
-    finish_hidden(1)
+    forward_hidden(1)
     loads["ck"].wait()
     loads["cv"].wait()
     attention()
-    forward_hidden(1)
+    pass_on(3)
+    finish_hidden(2)
+    forward_far(1)
     loads["down"].wait()
     down(0)
-    finish_hidden(2)
     attended_spread()
     forward_hidden(2)
-    down(1)
     finish_hidden(3)
     attended_forward()
+    down(1)
+    forward_far(2)
+    forward_hidden(3)
+    attended_far()
     down(2)
-    forward_hidden(3)
     loads["out"].wait()
-    for k in range(4):
-        attc[k].wait_recv()
+    wait_attended()
     out_product(0)
     out_product(1)
     out_product(2)
+    forward_far(3)
     down(3)
     out_product(3)
 
@@ -435,25 +506,27 @@
             jax.ShapeDtypeStruct((BLK, DEPTH), BF16),
             jax.ShapeDtypeStruct((OWN, 2 * HEAD), BF16),
         ),
-        in_specs=[vm, vm, sm, vm, hb, hb, hb, hb, vm, hb, hb, hb],
+        in_specs=[hb, hb, sm, hb, hb, hb, hb, hb, hb, hb, hb, hb],
         out_specs=(vm, vm),
         scratch_shapes=[
+            v((BLK, DEPTH), BF16), v((1, DEPTH), F32), v((1, HEAD), F32), v((PAIR, DEPTH), BF16),
             v((DEPTH, HID), BF16), v((DEPTH, HID), BF16), v((HID, DEPTH), BF16),
             v((DEPTH, QC), BF16), v((QC, DEPTH), BF16),
             v((OWN, SLOTS, HEAD), BF16), v((OWN, SLOTS, HEAD), BF16), v((DEPTH, 128), BF16),
             v((8, 8, 128), F32), v((16, BLK, DEPTH), BF16),
             v((T, 2, 4, PIECE, 512), BF16), v((T, 4, PIECE, 512), BF16),
-            v((T, 4, PIECE, 512), BF16), v((T, 3, PIECE, 512), BF16), v((T, PIECE, HID), BF16),
+            v((T, 4, PIECE, 512), BF16), v((T, 2, 64, 512), BF16), v((T, 6, 64, 512), BF16),
+            v((T, PIECE, HID), BF16),
             v((2, 4, 2, BLK, QC + 128), F32), v((4, 2, BLK, QC + 128), F32),
-            v((4, 2, BLK, QC + 128), F32), v((3, 2, BLK, QC + 128), F32),
+            v((4, 2, BLK, QC + 128), F32), v((2, BLK, QC + 128), F32), v((6, BLK, QC + 128), F32),
             v((2, 64, HEAD), F32), v((16, 8, 384), F32), v((16, 8, 384), F32),
             v((OWN, 32, HEAD), BF16), v((8, 2 * HEAD), F32), v((OWN, 32, HEAD), BF16),
             v((16, 8, HEAD), F32), v((16, 8, HEAD), F32), v((8, 64, QC), BF16),
             v((T, PIECE, DEPTH), F32), v((T, 4, BLK, DEPTH), BF16), v((16, BLK, DEPTH), BF16),
-            dma((7,)), dma((8,)), dma((8,)), dma((16,)), dma((16,)), dma((T,)), dma((T,)),
-            dma((T, 3)), dma((T, 3)), dma((T, 3)), dma((T, 3)), dma((T, 4)), dma((T, 4)),
-            dma((1,)), dma((1,)), dma((3,)), dma((3,)), dma((16,)), dma((16,)),
-            dma((16,)), dma((16,)), dma((3,)), dma((3,)), dma((4,)), dma((4,)),
+            dma((11,)), dma((8,)), dma((8,)), dma((16,)), dma((16,)), dma((T,)), dma((T,)),
+            dma((T, 6)), dma((T, 6)), dma((T, 4)), dma((T, 4)), dma((T, 4)), dma((T, 4)),
+            dma((1,)), dma((1,)), dma((6,)), dma((6,)), dma((16,)), dma((16,)),
+            dma((16,)), dma((16,)), dma((4,)), dma((4,)), dma((4,)), dma((4,)),
             dma((16,)), dma((16,)),
         ],
         compiler_params=pltpu.CompilerParams(
@@ -465,7 +538,7 @@
         name="layer",
     )(
         tokens, gain.reshape(1, DEPTH), lengths, jnp.asarray(freq), gate_weight, up_weight,
-        down_weight, query_weight, pair_weight, out_weight, cache_k, cache_v,
+        down_weight, query_weight, pair_weight.T, out_weight, cache_k, cache_v,
     )
 
 

time: 97.3 us -> 87.7 us (0.901); the launches traced: 95.4 us -> 87.5 us
  Pallas kernels: 90.3 us -> 84.2 us
  local copies, waits for them, and re-layouts: 4.42 us -> 2.75 us
    pallas_call x1, Pallas kernels: 90.3 us -> 84.2 us  [local(): pl.pallas_call(kernel, out_shape=(jax.ShapeDtypeStruct((BLK, DEPTH), BF16...]
    unnamed x3 -> x2, local copies, waits for them, and re-layouts: 4.42 us -> 2.75 us
where the time goes in v2:
time: 87.7 us; the launch traced here: 87.5 us
  Pallas kernels  84.2 us (96%)
  local copies, waits for them, and re-layouts  2.75 us (3%)
    pallas_call x1, Pallas kernels, local(): pl.pallas_call(kernel, out_shape=(jax.ShapeDtypeStruct((BLK, DEPTH), BF16...  84.2 us
    unnamed x2, local copies, waits for them, and re-layouts  2.75 us

profile of v2, /device:TPU:1, one launch (start us, length us, event | category | flops | bytes accessed | tf_op | source)
XLA Modules:
  0.0 87.5 jit_solution(2030013744002223865)
XLA Ops:
  0.6 84.2 %layer.1 = (bf16[32,1024]{1,0:T(8,128)(2,1)}, bf16[4,512]{1,0:T(4,128)(2,1)}) custom-call(bf16[32,1024]{1,0:T(8,128)(2,1)} %tokens_h.1, f32[1,1024]{1,0:T(1,128)} %bitcast.3, s32[64]{0:T(128)} %lengths.1, f32[1,256]{1,0:T(1,128)} %constant.2.clone.freq_h, bf16[1024,2048]{1,0:T(8,128)(2,1)} %gate_h.1, bf16[1024,2048]{1,0:T(8,128)(2,1)} %up_h.1, ...), custom_call_target="tpu_custom_call" | custom-call | flops 7549747200 | bytes 20971520 | tf_op jit(solution)/shard_map/layer/pallas_call | solution.py:503
  84.8 1.5 %copy.16 = bf16[32,1024]{1,0:T(8,128)(2,1)} copy(bf16[32,1024]{1,0:T(8,128)(2,1)} %get-tuple-element.4) | data formatting | bytes 131072
  86.3 1.3 %copy.17 = bf16[4,512]{1,0:T(4,128)(2,1)} copy(bf16[4,512]{1,0:T(4,128)(2,1)} %get-tuple-element.5) | data formatting | bytes 8192

commit v3 on v2

--- a/solution.py
+++ b/solution.py
@@ -41,10 +41,10 @@
     mixed, new_pair,
     tokens, gain, freq, pair_w,
     gate_w, up_w, down_w, query_w, out_w, ck, cv, pair_p,
-    st, xb, part, corecv, zs, zsum, zrecv, hid,
+    st, sst, tokb, xb, part, corecv, zs, zsum, zrecv, hid,
     qpart, qcore, qsum, qfwd, qz, tab, ab, arecv, qall, npair, attk, bb, brecv, att,
     total, dpart, rs,
-    lsem, st_s, st_r, tok_s, tok_r, core_s, core_r, z_s, z_r, agz_s, agz_r, agc_s, agc_r,
+    lsem, st_s, st_r, ss_s, ss_r, tok_s, tok_r, core_s, core_r, z_s, z_r, agz_s, agz_r, agc_s, agc_r,
     qc_s, qc_r, qz_s, qz_r, a_s, a_r, b_s, b_r, attz_s, attz_r, attc_s, attc_r, rs_s, rs_r,
 ):
     i = lax.axis_index("gx")
@@ -82,7 +82,23 @@
     for k in range(1, 16):
         pl.semaphore_signal(barrier, inc=1, device_id=(i, (j + k) % 16), device_id_type=MESH)
 
+    peers = {}
+    for t in range(T):
+        for dy in range(4):
+            dx = (t - dy) % 4
+            if dx or dy:
+                peers[4 * t + dy] = (i, ((y + 4 - dy) % 4) * 4 + (x + 4 - dx) % 4)
+    toks, stats = {}, {}
+
+    def send_tokens(t):
+        for b in range(4 * t, 4 * t + 4):
+            if b in peers:
+                toks[b] = send(tokens, tokb.at[b], tok_s.at[b], tok_r.at[b], peers[b])
+
     loads["tokens"].wait()
+    pl.semaphore_wait(barrier, 22)
+    send_tokens(0)
+
     values = tokens[...].astype(F32)
     mean_l = jnp.sum(values, axis=1, keepdims=True) * (1.0 / DEPTH)
     off = values - mean_l
@@ -97,11 +113,10 @@
 
     sub = iota((8, 128), 0)
     st[0] = jnp.where(sub == 0, to_row(mean_l), jnp.where(sub == 1, to_row(dev_l), 0.0))
-    pl.semaphore_wait(barrier, 22)
-
     cps = []
     for k in range(1, 8):
         cps.append(send(st.at[0], st.at[k], st_s.at[k], st_r.at[k], ((i + k) % 8, j)))
+    send_tokens(1)
 
     place = onehot(iota((PAIR, 128), 1) == iota((PAIR, 128), 0) + PAIR * (j % 4))
     loads["pair"].wait()
@@ -123,17 +138,17 @@
         gap = means[k] - mean
         spread = spread + (st[k, 1:2, :] + DEPTH * (gap * gap))
     scale = lax.rsqrt(spread * (1.0 / WIDTH) + EPS)
-    xb[0] = ((values - to_col(mean)) * to_col(scale) * gain[...]).astype(BF16)
-
-    toks = {}
-    for t in range(T):
-        for dy in range(4):
-            dx = (t - dy) % 4
-            if dx == 0 and dy == 0:
-                continue
-            dst = (i, ((y + 4 - dy) % 4) * 4 + (x + 4 - dx) % 4)
-            b = 4 * t + dy
-            toks[b] = send(xb.at[0], xb.at[b], tok_s.at[b], tok_r.at[b], dst)
+    sst[0] = jnp.where(sub == 0, mean, jnp.where(sub == 1, scale, 0.0))
+    for b in peers:
+        stats[b] = send(sst.at[0], sst.at[b], ss_s.at[b], ss_r.at[b], peers[b])
+    send_tokens(2)
+    send_tokens(3)
+
+    def normalize(b, rows):
+        centered = rows.astype(F32) - to_col(sst[b, 0:1, :])
+        xb[b] = (centered * to_col(sst[b, 1:2, :]) * gain[...]).astype(BF16)
+
+    normalize(0, tokens[...])
 
     lens = jnp.zeros((64, 128), jnp.int32)
     row64 = iota((64, 128), 0)
@@ -145,16 +160,18 @@
     tab[1] = jnp.sin(angle)
 
     def wait_tokens(t):
-        for dy in range(4):
-            if 4 * t + dy in toks:
-                toks[4 * t + dy].wait_recv()
+        for b in range(4 * t, 4 * t + 4):
+            if b in toks:
+                toks[b].wait_recv()
+                stats[b].wait_recv()
+                normalize(b, tokb[b])
 
     def piece_rows(t):
         return xb[4 * t : 4 * t + 4].reshape(PIECE, DEPTH)
 
     core = {}
 
-    def gate_up(t):
+    def gate_up(t, which):
         def half(cc):
             def body(k, carry):
                 rows = piece_rows(t)
@@ -167,9 +184,11 @@
 
             lax.fori_loop(0, 4, body, 0)
 
-        half(1 - c)
-        core[t] = send(part.at[t, 1 - c], corecv.at[t], core_s.at[t], core_r.at[t], sib)
-        half(c)
+        if which == "give":
+            half(1 - c)
+            core[t] = send(part.at[t, 1 - c], corecv.at[t], core_s.at[t], core_r.at[t], sib)
+        else:
+            half(c)
 
     zcp = {}
 
@@ -250,17 +269,18 @@
 
     qcp = {}
 
-    def query_product():
-        for t in range(T):
-            rows = piece_rows(t)
-            q = dot(rows, query_w[...])
-            p = dot(rows, pair_p[...])
-            for dy in range(4):
-                zz = (y + dy) % 4
-                xx = (x + (t - dy) % 4) % 4
-                piece = slice(BLK * dy, BLK * dy + BLK)
-                qpart[xx // 2, zz, xx % 2, :, 0:QC] = q[piece]
-                qpart[xx // 2, zz, xx % 2, :, QC:] = p[piece]
+    def query_product(t):
+        rows = piece_rows(t)
+        q = dot(rows, query_w[...])
+        p = dot(rows, pair_p[...])
+        for dy in range(4):
+            zz = (y + dy) % 4
+            xx = (x + (t - dy) % 4) % 4
+            piece = slice(BLK * dy, BLK * dy + BLK)
+            qpart[xx // 2, zz, xx % 2, :, 0:QC] = q[piece]
+            qpart[xx // 2, zz, xx % 2, :, QC:] = p[piece]
+
+    def query_send():
         qcp["core"] = send(qpart.at[1 - c], qcore, qc_s.at[0], qc_r.at[0], sib)
 
     def query_core_add():
@@ -382,26 +402,15 @@
             )
             att[i, :, HEAD * h : HEAD * h + HEAD] = dot(gather, rows).astype(BF16)
         block = att.at[i]
-        attz[0] = send(block, block, attz_s.at[0], attz_r.at[0], up_dev)
-        attz[1] = send(block, block, attz_s.at[1], attz_r.at[1], dn_dev)
-        attc[0] = send(block, block, attc_s.at[0], attc_r.at[0], sib)
+        for n, k in enumerate((1, 3, 2)):
+            attz[n] = send(block, block, attz_s.at[n], attz_r.at[n], zdev(k))
+        attc[3] = send(block, block, attc_s.at[3], attc_r.at[3], sib)
 
     def attended_forward():
-        for n, (k, half, dev) in enumerate(
-            ((1, slice(0, 32), up_dev), (3, slice(32, 64), dn_dev))
-        ):
+        for n, k in enumerate((1, 3, 2)):
             attz[n].wait_recv()
-            part_of = att.at[((z + 4 - k) % 4) * 2 + c, half]
-            attz[2 + n] = send(part_of, part_of, attz_s.at[2 + n], attz_r.at[2 + n], dev)
-        for n, k in ((1, 1), (2, 3)):
             block = att.at[((z + 4 - k) % 4) * 2 + c]
             attc[n] = send(block, block, attc_s.at[n], attc_r.at[n], sib)
-
-    def attended_far():
-        attz[2].wait_recv()
-        attz[3].wait_recv()
-        block = att.at[far * 2 + c]
-        attc[3] = send(block, block, attc_s.at[3], attc_r.at[3], sib)
 
     rcp = {}
 
@@ -431,46 +440,53 @@
     loads["gate"].wait()
     loads["up"].wait()
     wait_tokens(0)
-    gate_up(0)
+    gate_up(0, "give")
+    gate_up(0, "keep")
     core_add(0)
+    loads["query"].wait()
+    query_product(0)
     wait_tokens(1)
-    gate_up(1)
+    query_product(1)
+    wait_tokens(2)
+    query_product(2)
+    wait_tokens(3)
+    query_product(3)
+    query_send()
+    pass_on(0)
+    gate_up(1, "give")
+    query_core_add()
+    gate_up(1, "keep")
+    gate_up(2, "give")
+    query_pass_on()
     core_add(1)
-    pass_on(0)
-    wait_tokens(2)
-    wait_tokens(3)
-    loads["query"].wait()
-    query_product()
+    finish_hidden(0)
+    gate_up(2, "keep")
+    core_add(2)
+    gate_up(3, "give")
+    query_finish()
     pass_on(1)
-    query_core_add()
-    finish_hidden(0)
-    gate_up(2)
-    query_pass_on()
-    core_add(2)
+    gate_up(3, "keep")
+    core_add(3)
     forward_hidden(0)
-    finish_hidden(1)
-    gate_up(3)
-    query_finish()
     pass_on(2)
-    forward_far(0)
-    core_add(3)
-    forward_hidden(1)
     loads["ck"].wait()
     loads["cv"].wait()
     attention()
+    finish_hidden(1)
     pass_on(3)
+    forward_far(0)
+    forward_hidden(1)
     finish_hidden(2)
-    forward_far(1)
     loads["down"].wait()
     down(0)
     attended_spread()
+    finish_hidden(3)
+    forward_far(1)
     forward_hidden(2)
-    finish_hidden(3)
+    down(1)
     attended_forward()
-    down(1)
     forward_far(2)
     forward_hidden(3)
-    attended_far()
     down(2)
     loads["out"].wait()
     wait_attended()
@@ -513,7 +529,8 @@
             v((DEPTH, HID), BF16), v((DEPTH, HID), BF16), v((HID, DEPTH), BF16),
             v((DEPTH, QC), BF16), v((QC, DEPTH), BF16),
             v((OWN, SLOTS, HEAD), BF16), v((OWN, SLOTS, HEAD), BF16), v((DEPTH, 128), BF16),
-            v((8, 8, 128), F32), v((16, BLK, DEPTH), BF16),
+            v((8, 8, 128), F32), v((16, 8, 128), F32), v((16, BLK, DEPTH), BF16),
+            v((16, BLK, DEPTH), BF16),
             v((T, 2, 4, PIECE, 512), BF16), v((T, 4, PIECE, 512), BF16),
             v((T, 4, PIECE, 512), BF16), v((T, 2, 64, 512), BF16), v((T, 6, 64, 512), BF16),
             v((T, PIECE, HID), BF16),
@@ -523,7 +540,8 @@
             v((OWN, 32, HEAD), BF16), v((8, 2 * HEAD), F32), v((OWN, 32, HEAD), BF16),
             v((16, 8, HEAD), F32), v((16, 8, HEAD), F32), v((8, 64, QC), BF16),
             v((T, PIECE, DEPTH), F32), v((T, 4, BLK, DEPTH), BF16), v((16, BLK, DEPTH), BF16),
-            dma((11,)), dma((8,)), dma((8,)), dma((16,)), dma((16,)), dma((T,)), dma((T,)),
+            dma((11,)), dma((8,)), dma((8,)), dma((16,)), dma((16,)), dma((16,)), dma((16,)),
+            dma((T,)), dma((T,)),
             dma((T, 6)), dma((T, 6)), dma((T, 4)), dma((T, 4)), dma((T, 4)), dma((T, 4)),
             dma((1,)), dma((1,)), dma((6,)), dma((6,)), dma((16,)), dma((16,)),
             dma((16,)), dma((16,)), dma((4,)), dma((4,)), dma((4,)), dma((4,)),

time: 87.7 us -> 84.4 us (0.962)
  Pallas kernels: 84.2 us -> 80.8 us
    pallas_call x1, Pallas kernels: 84.2 us -> 80.8 us  [local(): pl.pallas_call(kernel, out_shape=(jax.ShapeDtypeStruct((BLK, DEPTH), BF16...]
where the time goes in v3:
time: 84.4 us; the launch traced here: 84.2 us
  Pallas kernels  80.8 us (96%)
  local copies, waits for them, and re-layouts  2.75 us (3%)
    pallas_call x1, Pallas kernels, local(): pl.pallas_call(kernel, out_shape=(jax.ShapeDtypeStruct((BLK, DEPTH), BF16...  80.8 us
    unnamed x2, local copies, waits for them, and re-layouts  2.75 us

profile of v3, /device:TPU:1, one launch (start us, length us, event | category | flops | bytes accessed | tf_op | source)
XLA Modules:
  0.0 84.2 jit_solution(13911462223525612655)
XLA Ops:
  0.6 80.8 %layer.1 = (bf16[32,1024]{1,0:T(8,128)(2,1)}, bf16[4,512]{1,0:T(4,128)(2,1)}) custom-call(bf16[32,1024]{1,0:T(8,128)(2,1)} %tokens_h.1, f32[1,1024]{1,0:T(1,128)} %bitcast.3, s32[64]{0:T(128)} %lengths.1, f32[1,256]{1,0:T(1,128)} %constant.2.clone.freq_h, bf16[1024,2048]{1,0:T(8,128)(2,1)} %gate_h.1, bf16[1024,2048]{1,0:T(8,128)(2,1)} %up_h.1, ...), custom_call_target="tpu_custom_call" | custom-call | flops 7549747200 | bytes 20971520 | tf_op jit(solution)/shard_map/layer/pallas_call | solution.py:519
  81.4 1.5 %copy.16 = bf16[32,1024]{1,0:T(8,128)(2,1)} copy(bf16[32,1024]{1,0:T(8,128)(2,1)} %get-tuple-element.4) | data formatting | bytes 131072
  82.9 1.3 %copy.17 = bf16[4,512]{1,0:T(4,128)(2,1)} copy(bf16[4,512]{1,0:T(4,128)(2,1)} %get-tuple-element.5) | data formatting | bytes 8192

commit v4 on v3

--- a/solution.py
+++ b/solution.py
@@ -43,9 +43,10 @@
     gate_w, up_w, down_w, query_w, out_w, ck, cv, pair_p,
     st, sst, tokb, xb, part, corecv, zs, zsum, zrecv, hid,
     qpart, qcore, qsum, qfwd, qz, tab, ab, arecv, qall, npair, attk, bb, brecv, att,
-    total, dpart, rs,
-    lsem, st_s, st_r, ss_s, ss_r, tok_s, tok_r, core_s, core_r, z_s, z_r, agz_s, agz_r, agc_s, agc_r,
-    qc_s, qc_r, qz_s, qz_r, a_s, a_r, b_s, b_r, attz_s, attz_r, attc_s, attc_r, rs_s, rs_r,
+    total, dpart, r1x, r1y, r2x, r2y, mid,
+    lsem, st_s, st_r, ss_s, ss_r, tok_s, tok_r, toka_s, toka_r, core_s, core_r, z_s, z_r, agz_s, agz_r, agc_s, agc_r,
+    qc_s, qc_r, qz_s, qz_r, a_s, a_r, b_s, b_r, attz_s, attz_r, attc_s, attc_r,
+    r1x_s, r1x_r, r1y_s, r1y_r, r2x_s, r2x_r, r2y_s, r2y_r,
 ):
     i = lax.axis_index("gx")
     j = lax.axis_index("gy")
@@ -90,14 +91,38 @@
                 peers[4 * t + dy] = (i, ((y + 4 - dy) % 4) * 4 + (x + 4 - dx) % 4)
     toks, stats = {}, {}
 
-    def send_tokens(t):
-        for b in range(4 * t, 4 * t + 4):
-            if b in peers:
-                toks[b] = send(tokens, tokb.at[b], tok_s.at[b], tok_r.at[b], peers[b])
+    top, low = slice(0, 16), slice(16, 32)
+
+    def place_of(dx, dy):
+        return 4 * ((dx + dy) % 4) + dy
+
+    def send_tokens():
+        for d in (2, 1, 3):
+            for b in (place_of(d, 0), place_of(0, d)):
+                toks[b] = [send(tokens, tokb.at[b], tok_s.at[b], tok_r.at[b], peers[b])]
+
+    def forward_tokens():
+        for d in (1, 3, 2):
+            toks[place_of(d, 0)][0].wait_recv()
+            toks[place_of(0, d)][0].wait_recv()
+        for t in range(T):
+            for dy in (1, 2, 3):
+                dx = (t - dy) % 4
+                if dx == 0:
+                    continue
+                b, bx, by = place_of(dx, dy), place_of(dx, 0), place_of(0, dy)
+                toks[b] = [
+                    send(
+                        tokb.at[bx, top], tokb.at[b, top], toka_s.at[b, 0], toka_r.at[b, 0],
+                        peers[by],
+                    ),
+                    send(
+                        tokb.at[by, low], tokb.at[b, low], toka_s.at[b, 1], toka_r.at[b, 1],
+                        peers[bx],
+                    ),
+                ]
 
     loads["tokens"].wait()
-    pl.semaphore_wait(barrier, 22)
-    send_tokens(0)
 
     values = tokens[...].astype(F32)
     mean_l = jnp.sum(values, axis=1, keepdims=True) * (1.0 / DEPTH)
@@ -113,10 +138,11 @@
 
     sub = iota((8, 128), 0)
     st[0] = jnp.where(sub == 0, to_row(mean_l), jnp.where(sub == 1, to_row(dev_l), 0.0))
+    pl.semaphore_wait(barrier, 22)
     cps = []
     for k in range(1, 8):
         cps.append(send(st.at[0], st.at[k], st_s.at[k], st_r.at[k], ((i + k) % 8, j)))
-    send_tokens(1)
+    send_tokens()
 
     place = onehot(iota((PAIR, 128), 1) == iota((PAIR, 128), 0) + PAIR * (j % 4))
     loads["pair"].wait()
@@ -141,8 +167,7 @@
     sst[0] = jnp.where(sub == 0, mean, jnp.where(sub == 1, scale, 0.0))
     for b in peers:
         stats[b] = send(sst.at[0], sst.at[b], ss_s.at[b], ss_r.at[b], peers[b])
-    send_tokens(2)
-    send_tokens(3)
+    forward_tokens()
 
     def normalize(b, rows):
         centered = rows.astype(F32) - to_col(sst[b, 0:1, :])
@@ -162,7 +187,8 @@
     def wait_tokens(t):
         for b in range(4 * t, 4 * t + 4):
             if b in toks:
-                toks[b].wait_recv()
+                for cp in toks[b][0 if len(toks[b]) == 2 else 1 :]:
+                    cp.wait_recv()
                 stats[b].wait_recv()
                 normalize(b, tokb[b])
 
@@ -412,7 +438,13 @@
             block = att.at[((z + 4 - k) % 4) * 2 + c]
             attc[n] = send(block, block, attc_s.at[n], attc_r.at[n], sib)
 
-    rcp = {}
+    r1 = {}
+
+    def along_x(d):
+        return (i, y * 4 + (x + d) % 4)
+
+    def along_y(d):
+        return (i, ((y + d) % 4) * 4 + x)
 
     def wait_attended():
         for k in range(4):
@@ -431,11 +463,22 @@
             dpart[t, :, :, cols] = v.astype(BF16).reshape(4, BLK, 512)
         for dy in range(4):
             dx = (t - dy) % 4
-            if dx == 0 and dy == 0:
-                continue
-            b = 4 * t + dy
-            dst = (i, ((y + dy) % 4) * 4 + (x + dx) % 4)
-            rcp[b] = send(dpart.at[t, dy], rs.at[b], rs_s.at[b], rs_r.at[b], dst)
+            if dx:
+                r1[0, dx, dy] = send(
+                    dpart.at[t, dy, top], r1x.at[dx, dy], r1x_s.at[dx, dy], r1x_r.at[dx, dy], along_x(dx)
+                )
+            if dy:
+                r1[1, dy, dx] = send(
+                    dpart.at[t, dy, low], r1y.at[dy, dx], r1y_s.at[dy, dx], r1y_r.at[dy, dx], along_y(dy)
+                )
+
+    def gathered(axis, d):
+        rows, recv = (top, r1x) if axis == 0 else (low, r1y)
+        v = dpart[d, d if axis == 0 else 0, rows].astype(F32)
+        for e in (1, 2, 3):
+            r1[axis, e, d].wait_recv()
+            v = v + recv[e, d].astype(F32)
+        return v
 
     loads["gate"].wait()
     loads["up"].wait()
@@ -497,11 +540,18 @@
     down(3)
     out_product(3)
 
-    result = tokens[...].astype(F32) + dpart[0, 0].astype(F32)
-    for b in range(1, 16):
-        rcp[b].wait_recv()
-        result = result + rs[b].astype(F32)
-    mixed[...] = result.astype(BF16)
+    r2 = {}
+    for d in (2, 1, 3):
+        mid[0, d] = gathered(0, d).astype(BF16)
+        r2[0, d] = send(mid.at[0, d], r2x.at[d], r2x_s.at[d], r2x_r.at[d], along_y(d))
+        mid[1, d] = gathered(1, d).astype(BF16)
+        r2[1, d] = send(mid.at[1, d], r2y.at[d], r2y_s.at[d], r2y_r.at[d], along_x(d))
+    for axis, (rows, recv) in enumerate(((top, r2x), (low, r2y))):
+        result = tokens[rows, :].astype(F32) + gathered(axis, 0)
+        for d in (1, 3, 2):
+            r2[axis, d].wait_recv()
+            result = result + recv[d].astype(F32)
+        mixed[rows, :] = result.astype(BF16)
     for cp in pending:
         cp.wait_send()
 
@@ -539,13 +589,15 @@
             v((2, 64, HEAD), F32), v((16, 8, 384), F32), v((16, 8, 384), F32),
             v((OWN, 32, HEAD), BF16), v((8, 2 * HEAD), F32), v((OWN, 32, HEAD), BF16),
             v((16, 8, HEAD), F32), v((16, 8, HEAD), F32), v((8, 64, QC), BF16),
-            v((T, PIECE, DEPTH), F32), v((T, 4, BLK, DEPTH), BF16), v((16, BLK, DEPTH), BF16),
+            v((T, PIECE, DEPTH), F32), v((T, 4, BLK, DEPTH), BF16), v((4, 4, 16, DEPTH), BF16),
+            v((4, 4, 16, DEPTH), BF16), v((4, 16, DEPTH), BF16), v((4, 16, DEPTH), BF16),
+            v((2, 4, 16, DEPTH), BF16),
             dma((11,)), dma((8,)), dma((8,)), dma((16,)), dma((16,)), dma((16,)), dma((16,)),
-            dma((T,)), dma((T,)),
+            dma((16, 2)), dma((16, 2)), dma((T,)), dma((T,)),
             dma((T, 6)), dma((T, 6)), dma((T, 4)), dma((T, 4)), dma((T, 4)), dma((T, 4)),
             dma((1,)), dma((1,)), dma((6,)), dma((6,)), dma((16,)), dma((16,)),
             dma((16,)), dma((16,)), dma((4,)), dma((4,)), dma((4,)), dma((4,)),
-            dma((16,)), dma((16,)),
+            dma((4, 4)), dma((4, 4)), dma((4, 4)), dma((4, 4)), dma((4,)), dma((4,)), dma((4,)), dma((4,)),
         ],
         compiler_params=pltpu.CompilerParams(
             collective_id=0, has_side_effects=True, vmem_limit_bytes=56 * 1024 * 1024

time: 84.4 us -> 81.6 us (0.967)
  Pallas kernels: 80.8 us -> 78 us
    pallas_call x1, Pallas kernels: 80.8 us -> 78 us  [local(): pl.pallas_call(kernel, out_shape=(jax.ShapeDtypeStruct((BLK, DEPTH), BF16...]
where the time goes in v4:
time: 81.6 us; the launch traced here: 81.4 us
  Pallas kernels  78 us (96%)
  local copies, waits for them, and re-layouts  2.75 us (3%)
    pallas_call x1, Pallas kernels, local(): pl.pallas_call(kernel, out_shape=(jax.ShapeDtypeStruct((BLK, DEPTH), BF16...  78 us
    unnamed x2, local copies, waits for them, and re-layouts  2.75 us

profile of v4, /device:TPU:1, one launch (start us, length us, event | category | flops | bytes accessed | tf_op | source)
XLA Modules:
  0.0 81.4 jit_solution(6594626496945528723)
XLA Ops:
  0.6 78.0 %layer.1 = (bf16[32,1024]{1,0:T(8,128)(2,1)}, bf16[4,512]{1,0:T(4,128)(2,1)}) custom-call(bf16[32,1024]{1,0:T(8,128)(2,1)} %tokens_h.1, f32[1,1024]{1,0:T(1,128)} %bitcast.3, s32[64]{0:T(128)} %lengths.1, f32[1,256]{1,0:T(1,128)} %constant.2.clone.freq_h, bf16[1024,2048]{1,0:T(8,128)(2,1)} %gate_h.1, bf16[1024,2048]{1,0:T(8,128)(2,1)} %up_h.1, ...), custom_call_target="tpu_custom_call" | custom-call | flops 7549747200 | bytes 20971520 | tf_op jit(solution)/shard_map/layer/pallas_call | solution.py:569
  78.7 1.5 %copy.16 = bf16[32,1024]{1,0:T(8,128)(2,1)} copy(bf16[32,1024]{1,0:T(8,128)(2,1)} %get-tuple-element.4) | data formatting | bytes 131072
  80.1 1.3 %copy.17 = bf16[4,512]{1,0:T(4,128)(2,1)} copy(bf16[4,512]{1,0:T(4,128)(2,1)} %get-tuple-element.5) | data formatting | bytes 8192

commit v5 on v4

--- a/solution.py
+++ b/solution.py
@@ -528,13 +528,13 @@
     forward_hidden(2)
     down(1)
     attended_forward()
-    forward_far(2)
     forward_hidden(3)
-    down(2)
     loads["out"].wait()
     wait_attended()
     out_product(0)
     out_product(1)
+    forward_far(2)
+    down(2)
     out_product(2)
     forward_far(3)
     down(3)

time: 81.6 us -> 81.3 us (level)
  no operation moved by 1% of the time
where the time goes in v5:
time: 81.3 us; the launch traced here: 81.1 us
  Pallas kernels  77.7 us (96%)
  local copies, waits for them, and re-layouts  2.75 us (3%)
    pallas_call x1, Pallas kernels, local(): pl.pallas_call(kernel, out_shape=(jax.ShapeDtypeStruct((BLK, DEPTH), BF16...  77.7 us
    unnamed x2, local copies, waits for them, and re-layouts  2.75 us

profile of v5, /device:TPU:1, one launch (start us, length us, event | category | flops | bytes accessed | tf_op | source)
XLA Modules:
  0.0 81.1 jit_solution(13968333190705825674)
XLA Ops:
  0.6 77.7 %layer.1 = (bf16[32,1024]{1,0:T(8,128)(2,1)}, bf16[4,512]{1,0:T(4,128)(2,1)}) custom-call(bf16[32,1024]{1,0:T(8,128)(2,1)} %tokens_h.1, f32[1,1024]{1,0:T(1,128)} %bitcast.3, s32[64]{0:T(128)} %lengths.1, f32[1,256]{1,0:T(1,128)} %constant.2.clone.freq_h, bf16[1024,2048]{1,0:T(8,128)(2,1)} %gate_h.1, bf16[1024,2048]{1,0:T(8,128)(2,1)} %up_h.1, ...), custom_call_target="tpu_custom_call" | custom-call | flops 7549747200 | bytes 20971520 | tf_op jit(solution)/shard_map/layer/pallas_call | solution.py:569
  78.4 1.5 %copy.16 = bf16[32,1024]{1,0:T(8,128)(2,1)} copy(bf16[32,1024]{1,0:T(8,128)(2,1)} %get-tuple-element.4) | data formatting | bytes 131072
  79.8 1.3 %copy.17 = bf16[4,512]{1,0:T(4,128)(2,1)} copy(bf16[4,512]{1,0:T(4,128)(2,1)} %get-tuple-element.5) | data formatting | bytes 8192
